TPU v7x, 512 devices: a whole 4x4x16 slice. The times are simulated.
512 devices in a mesh: pair: 128 (over y, z, core), red: 4 (over x).
Axes of the slice: x: 4, y: 4, z: 16, core: 2. Of those that a mesh axis runs over, the one named last changes fastest.
Arguments:
- amplitudes: bfloat16 [2048, 4096], P('pair', 'red'), may hold values from -6 to 6
- integrals: bfloat16 [4096, 65536], P('red', 'pair'), may hold values from -0.125 to 0.125
- pattern: int32 [128, 64], P('pair', 'red'), may hold values from 0 to 1, as said below
Outputs:
- ladder_term: bfloat16 [128, 16, 65536], P(None, 'red', 'pair')
Inputs may be any that keep to these rules, and one draw needn't show every extreme that they name: `pattern`: in every tile, exactly 8 of each aligned group of 16 blocks are 1.
All inputs are finite; a program needn't handle non-finite values.
Results may differ from a plain program's by a relative error of at most 0.0013.
Values may be sent and summed in bfloat16 or wider, within the bound.
A program may use at most 64 MiB of HBM per device.

v0:
```python
import jax
import jax.numpy as jnp
from jax import lax
from jax.sharding import PartitionSpec as P


def shards(amplitudes, integrals, pattern):
    tile_rows = amplitudes.shape[0]
    blocks = pattern.shape[1]
    block_width = amplitudes.shape[1] // blocks
    out_width = integrals.shape[1]
    keep_mask = jnp.repeat(jnp.repeat(pattern, tile_rows, axis=0), block_width, axis=1).astype(
        jnp.bfloat16
    )
    masked = amplitudes * keep_mask
    partial_value = jnp.dot(
        lax.all_gather(masked, "pair", axis=0, tiled=True),
        integrals,
        preferred_element_type=jnp.float32,
    )
    tile_count = partial_value.shape[0] // tile_rows
    summed = lax.psum_scatter(
        partial_value.reshape(tile_count, tile_rows, out_width),
        "red",
        scatter_dimension=1,
        tiled=True,
    )
    return summed.astype(jnp.bfloat16)


def solution(mesh):
    placed = (P("pair", "red"), P("red", "pair"), P("pair", "red"))
    return jax.shard_map(
        shards, mesh=mesh, in_specs=placed, out_specs=P(None, "red", "pair"), check_vma=False
    )
```

profile of v0, /device:TPU:1, one launch (start us, length us, event | category | flops | bytes accessed | tf_op | source)
XLA Modules:
  0.0 226.7 jit_solution(17842721416136384331)
XLA Ops:
  6.5 0.0 copy-start
  6.5 0.0 all-gather.2.cloned.1.call-start
  6.5 0.7 convert_bitcast_fusion
  7.3 0.1 broadcast_in_dim.6
  7.4 0.1 convert_element_type.16
  7.4 1.4 broadcast_multiply_fusion
  8.8 0.0 all-gather.2.cloned.1.call-update
  8.9 0.0 reduce-scatter.2.cloned.1.call-start
  8.9 149.4 %all-gather.2.cloned.1.call-done = bf16[2048,1024]{1,0:T(8,128)(2,1)} async-done(((bf16[16,1024]{1,0:T(8,128)(2,1)}), bf16[2048,1024]{1,0:T(8,128)(2,1)}) %all-gather.2.cloned.1.call-update) | async-done | bytes 4194320 | tf_op jit(solution)/shard_map/all_gather | solution.py:17
  158.3 0.0 copy-done
  158.3 4.5 %fusion = f32[2048,512]{1,0:T(8,128)S(1)} fusion(bf16[2048,1024]{1,0:T(8,128)(2,1)} %all-gather.2.cloned.1.call-done, bf16[1024,512]{1,0:T(8,128)(2,1)S(1)} %copy-done), kind=kOutput, calls=%fused_computation.2 | convolution fusion | flops 2147483648 | bytes 9437184 | tf_op jit(solution)/shard_map/dot_general | solution.py:16
  162.8 4.4 %copy.4 = f32[128,16,512]{2,0,1:T(8,128)} copy(f32[128,16,512]{2,1,0:T(8,128)S(1)} %bitcast.5) | data formatting | bytes 8388608 | tf_op jit(solution)/shard_map/reshape | solution.py:23
  167.2 0.0 reduce-scatter.2.cloned.1.call-update
  167.2 50.2 %reduce-scatter.2.cloned.1.call-done = f32[128,4,512]{2,0,1:T(8,128)} async-done(((f32[128,16,512]{2,0,1:T(8,128)}), f32[128,4,512]{2,0,1:T(8,128)}) %reduce-scatter.2.cloned.1.call-update) | async-done | bytes 1048592 | tf_op jit(solution)/shard_map/reduce_scatter | solution.py:22
  217.3 1.3 convert_element_type.17
  218.6 1.2 copy.5
Async XLA Ops:
  6.5 151.7 %copy-start = (bf16[1024,512]{1,0:T(8,128)(2,1)S(1)}, bf16[1024,512]{1,0:T(8,128)(2,1)}, u32[]{:S(2)}) copy-start(bf16[1024,512]{1,0:T(8,128)(2,1)} %param.4) | copy-start | bytes 3145732
  6.5 151.7 %all-gather.2.cloned.1.call-start = ((), (), s32[]{:S(2)}) async-start(), calls=%async_computation.1 | async-start | bytes 4227072 | tf_op jit(solution)/shard_map/all_gather | solution.py:17
  8.9 208.5 %reduce-scatter.2.cloned.1.call-start = ((), (), s32[]{:S(2)}) async-start(), calls=%async_computation.2 | async-start | bytes 5242880 | tf_op jit(solution)/shard_map/reduce_scatter | solution.py:22
Sparse Core Ops, SparseCore 0:
  10.5 147.7 all-gather.1
  167.3 49.9 reduce-scatter.1
where the time goes:
time: 227 us
  waiting for transfers between devices  200 us (88%)
  between operations  13.4 us (6%)
  local copies, waits for them, and re-layouts  5.73 us (3%)
  matrix products  4.53 us (2%)
  other arithmetic  3.41 us (2%)
    all_gather x1, waiting for transfers between devices, shards(): lax.all_gather(masked, 'pair', axis=0, tiled=True)  149 us
    reduce_scatter x1, waiting for transfers between devices, shards(): lax.psum_scatter(partial_value.reshape(tile_count, tile_rows, out_width),...  50.2 us
  transfers between devices with their start and end apart: 2, of which 2 were waited for; matrix products, arithmetic and copies ran while one was open for 0% of the time, Pallas kernels for 0%

commit v1 on v0

--- a/solution.py
+++ b/solution.py
@@ -14,7 +14,15 @@
     )
     masked = amplitudes * keep_mask
     partial_value = jnp.dot(
-        lax.all_gather(masked, "pair", axis=0, tiled=True),
+        jnp.concatenate(
+            jax.lax.all_to_all(
+                jnp.stack([masked] * jax.lax.axis_size("pair")),
+                split_axis=0,
+                axis_name="pair",
+                concat_axis=0,
+            ),
+            axis=0,
+        ),
         integrals,
         preferred_element_type=jnp.float32,
     )

time: 227 us -> 283 us (1.25)
  blocking collectives: 0 us -> 206 us
  waiting for transfers between devices: 200 us -> 51.5 us
  local copies, waits for them, and re-layouts: 5.73 us -> 1.89 us
    all_to_all x0 -> x1, blocking collectives: none -> 206 us  [shards(): jax.lax.all_to_all(jnp.stack([masked] * jax.lax.axis_size('pair')), split...]
    all_gather x1 -> x0, waiting for transfers between devices: 149 us -> none  [shards(): lax.all_gather(masked, 'pair', axis=0, tiled=True)]
    reshape x1 -> x0, local copies, waits for them, and re-layouts: 4.37 us -> none  [shards(): partial_value.reshape(tile_count, tile_rows, out_width)]
  transfers between devices with their start and end apart: 2 -> 1, of which waited for: 2 -> 1; matrix products, arithmetic and copies ran while one was open for 0% -> 0% of each run, Pallas kernels for 0% -> 0%
where the time goes in v1:
time: 283 us
  blocking collectives  206 us (73%)
  waiting for transfers between devices  51.5 us (18%)
  between operations  13.4 us (5%)
  matrix products  7.01 us (2%)
    all_to_all x1, blocking collectives, shards(): jax.lax.all_to_all(jnp.stack([masked] * jax.lax.axis_size('pair')), split...  206 us
    reduce_scatter x1, waiting for transfers between devices, shards(): lax.psum_scatter(partial_value.reshape(tile_count, tile_rows, out_width),...  51.5 us
    dot_general x1, matrix products, shards(): jnp.dot(jnp.concatenate(jax.lax.all_to_all(jnp.stack([masked] * jax.lax.a...  7.01 us
  transfers between devices with their start and end apart: 1, of which 1 were waited for; matrix products, arithmetic and copies ran while one was open for 0% of the time, Pallas kernels for 0%

profile of v1, /device:TPU:1, one launch (start us, length us, event | category | flops | bytes accessed | tf_op | source)
XLA Modules:
  0.0 282.6 jit_solution(10264506776064788397)
XLA Ops:
  6.5 0.0 copy-start
  6.5 0.0 reduce-scatter.2.cloned.1.call-start
  6.5 0.7 convert_bitcast_fusion
  7.3 0.1 broadcast_in_dim.6
  7.4 0.1 convert_element_type.16
  7.4 0.8 broadcast_multiply_fusion
  8.2 0.5 stack.2
  8.7 206.0 %all_to_all.5 = bf16[128,16,1024]{2,1,0:T(8,128)(2,1)S(1)} all-to-all(bf16[128,16,1024]{2,1,0:T(8,128)(2,1)S(1)} %stack.2), channel_id=1, replica_groups=mesh['pair'=128,'red'=4] {'pair'}, dimensions={0} | all-to-all | bytes 8388608 | tf_op jit(solution)/shard_map/all_to_all | solution.py:18
  214.7 0.0 copy-done
  214.7 7.0 %fusion = f32[128,16,512]{2,0,1:T(8,128)} fusion(bf16[128,16,1024]{2,1,0:T(8,128)(2,1)S(1)} %all_to_all.5, bf16[1024,512]{1,0:T(8,128)(2,1)S(1)} %copy-done), kind=kOutput, calls=%fused_computation | convolution fusion | flops 2147483648 | bytes 9437184 | tf_op jit(solution)/shard_map/dot_general | solution.py:16
  221.7 0.0 reduce-scatter.2.cloned.1.call-update
  221.8 51.5 %reduce-scatter.2.cloned.1.call-done = f32[128,4,512]{2,0,1:T(8,128)} async-done(((f32[128,16,512]{2,0,1:T(8,128)}), f32[128,4,512]{2,0,1:T(8,128)}) %reduce-scatter.2.cloned.1.call-update) | async-done | bytes 1048592 | tf_op jit(solution)/shard_map/reduce_scatter | solution.py:30
  273.3 1.3 convert_element_type.17
  274.6 1.2 copy.6
Async XLA Ops:
  6.5 208.2 %copy-start = (bf16[1024,512]{1,0:T(8,128)(2,1)S(1)}, bf16[1024,512]{1,0:T(8,128)(2,1)}, u32[]{:S(2)}) copy-start(bf16[1024,512]{1,0:T(8,128)(2,1)} %param.4) | copy-start | bytes 3145732
  6.5 266.8 %reduce-scatter.2.cloned.1.call-start = ((), (), s32[]{:S(2)}) async-start(), calls=%async_computation.2 | async-start | bytes 5242880 | tf_op jit(solution)/shard_map/reduce_scatter | solution.py:30
Sparse Core Ops, SparseCore 0:
  221.9 51.3 reduce-scatter.1
